TPU v7x, 256 devices: a whole 4x4x8 slice. The times are simulated.
256 devices in a mesh: seq: 16 (over z, core), head: 4 (over x), dp: 4 (over y).
Axes of the slice: x: 4, y: 4, z: 8, core: 2. Of those that a mesh axis runs over, the one named last changes fastest.
Arguments:
- self_queries: bfloat16 [4, 2048, 2560], P('dp', ('seq', 'head')), may hold values from -8 to 8
- self_keys: bfloat16 [4, 2048, 2560], P('dp', ('seq', 'head')), may hold values from -4 to 4
- self_values: bfloat16 [4, 2048, 2560], P('dp', ('seq', 'head')), may hold values from -6 to 6
- self_cotangent: bfloat16 [4, 2048, 2560], P('dp', ('seq', 'head')), may hold values from -6 to 6
- text_queries: bfloat16 [4, 4096, 2560], P('dp', 'seq', 'head'), may hold values from -8 to 8
- memory_keys: bfloat16 [4, 2048, 2560], P('dp', 'seq', 'head'), may hold values from -4 to 4
- memory_values: bfloat16 [4, 2048, 2560], P('dp', 'seq', 'head'), may hold values from -6 to 6
- text_cotangent: bfloat16 [4, 4096, 2560], P('dp', 'seq', 'head'), may hold values from -6 to 6
- slopes: float32 [2, 20], P(None, 'head'), may hold values from 0.01 to 0.3
- page_counts: int32 [4, 4], P('dp'), may hold values from 1 to 1024, as said below
- page_cols: int32 [4, 4], P('dp'), may hold values from 4 to 64
- text_page: int32 [4, 4096], P('dp'), may hold values from 0 to 3, as said below
Outputs:
- self_query_grad: bfloat16 [4, 2048, 2560], P('dp', ('seq', 'head'))
- self_key_grad: bfloat16 [4, 2048, 2560], P('dp', ('seq', 'head'))
- self_value_grad: bfloat16 [4, 2048, 2560], P('dp', ('seq', 'head'))
- slope_grad: float32 [2, 20], P(None, 'head')
- text_query_grad: bfloat16 [4, 4096, 2560], P('dp', 'seq', 'head')
- memory_key_grad: bfloat16 [4, 2048, 2560], P('dp', 'seq', 'head')
- memory_value_grad: bfloat16 [4, 2048, 2560], P('dp', 'seq', 'head')
Inputs may be any that keep to these rules, and one draw needn't show every extreme that they name: `page_counts`: each pack's counts sum to 2048; one page of every pack has exactly 1024 patches. `text_page`: never falls along a pack's text rows; every page has at least one text row.
All inputs are finite; a program needn't handle non-finite values.
Results may differ from a plain program's by a relative error of at most 0.006.
Values may be sent and summed in bfloat16 or wider, within the bound.
No kernel may reach another device: no remote copies, remote signals or barrier semaphores. Data moves between devices by JAX's collectives and lax.ppermute only.
A program may use at most 128 MiB of HBM per device.

v0:
```python
import jax
import jax.numpy as jnp
from jax import lax
from jax.sharding import PartitionSpec as P

MASK_FILL = -1e30


def page_layout(counts, widths, patch_total):
    page_ends = jnp.cumsum(counts)
    starts = page_ends - counts
    positions = jnp.arange(patch_total, dtype=jnp.int32)
    page_ids = jnp.sum((positions[:, None] >= page_ends[None, :]).astype(jnp.int32), axis=1)
    one_hot = page_ids[:, None] == jnp.arange(counts.shape[0], dtype=jnp.int32)[None, :]
    page_start = jnp.sum(jnp.where(one_hot, starts[None, :], 0), axis=1)
    page_width = jnp.sum(jnp.where(one_hot, widths[None, :], 0), axis=1)
    offsets = positions - page_start
    return (page_ids, offsets // page_width, offsets % page_width)


def take_rows(vector, row_start, row_count):
    return lax.dynamic_slice_in_dim(vector, row_start, row_count, 0)


def heads_of(matrix, head_count):
    return matrix.reshape(matrix.shape[0], head_count, -1)


def alibi(slopes, query_layout, key_layout):
    row_gap = jnp.abs(query_layout[1][:, None] - key_layout[1][None, :]).astype(jnp.float32)
    col_gap = jnp.abs(query_layout[2][:, None] - key_layout[2][None, :]).astype(jnp.float32)
    same_page = query_layout[0][:, None] == key_layout[0][None, :]
    decay = -(slopes[0][:, None, None] * row_gap[None] + slopes[1][:, None, None] * col_gap[None])
    return (jnp.where(same_page[None], decay, MASK_FILL), row_gap, col_gap)


def query_side(queries, key_rows, value_rows, grad_rows, logit_bias):
    inv_root = queries.shape[2] ** (-0.5)
    scores = (
        jnp.einsum("rhs,khs->hrk", queries, key_rows, preferred_element_type=jnp.float32) * inv_root
        + logit_bias
    )
    row_max = jnp.max(scores, axis=2, keepdims=True)
    weights = jnp.exp(scores - row_max)
    row_total = jnp.sum(weights, axis=2, keepdims=True)
    softmax_w = weights / row_total
    log_total = (row_max + jnp.log(row_total))[:, :, 0]
    grad_probs = jnp.einsum(
        "rhs,khs->hrk", grad_rows, value_rows, preferred_element_type=jnp.float32
    )
    row_delta = jnp.sum(softmax_w * grad_probs, axis=2, keepdims=True)
    grad_scores = softmax_w * (grad_probs - row_delta)
    grad_scores_b = grad_scores.astype(jnp.bfloat16)
    query_grad = (
        jnp.einsum("hrk,khs->rhs", grad_scores_b, key_rows, preferred_element_type=jnp.float32)
        * inv_root
    )
    return (
        query_grad,
        grad_scores,
        grad_scores_b,
        softmax_w.astype(jnp.bfloat16),
        log_total,
        row_delta[:, :, 0],
    )


def key_terms(grad_scores_b, softmax_b, queries, grad_rows, row_count):
    inv_root = queries.shape[3] ** (-0.5)
    key_grad = (
        jnp.einsum("chrk,crhs->khs", grad_scores_b, queries, preferred_element_type=jnp.float32)
        * inv_root
    )
    value_grad = jnp.einsum(
        "chrk,crhs->khs", softmax_b, grad_rows, preferred_element_type=jnp.float32
    )
    return jnp.stack([key_grad.reshape(row_count, -1), value_grad.reshape(row_count, -1)], axis=1)


def local(
    self_queries,
    self_keys,
    self_values,
    self_cotangent,
    text_queries,
    memory_keys,
    memory_values,
    text_cotangent,
    slopes,
    page_counts,
    page_cols,
    text_page,
):
    head_count = slopes.shape[1]
    regrouped = (
        lax.all_to_all(self_queries[0], "head", split_axis=1, concat_axis=0, tiled=True),
        lax.all_to_all(self_keys[0], "head", split_axis=1, concat_axis=0, tiled=True),
        lax.all_to_all(self_values[0], "head", split_axis=1, concat_axis=0, tiled=True),
        lax.all_to_all(self_cotangent[0], "head", split_axis=1, concat_axis=0, tiled=True),
    )
    local_queries, local_keys, local_values, local_grads = regrouped
    patch_rows = local_queries.shape[0]
    all_keys, all_values = (
        lax.all_gather(local_keys, "seq", axis=0, tiled=True),
        lax.all_gather(local_values, "seq", axis=0, tiled=True),
    )
    patch_total = all_keys.shape[0]
    whole_layout = page_layout(page_counts[0], page_cols[0], patch_total)
    own_start = lax.axis_index("seq") * patch_rows
    own_layout = tuple((take_rows(item, own_start, patch_rows) for item in whole_layout))
    self_bias, row_gap, col_gap = alibi(slopes, own_layout, whole_layout)
    query_heads = heads_of(local_queries, head_count)
    grad_heads = heads_of(local_grads, head_count)
    self_dq, self_ds, self_ds_b, self_p_b, self_lse, self_delta = query_side(
        query_heads,
        heads_of(all_keys, head_count),
        heads_of(all_values, head_count),
        grad_heads,
        self_bias,
    )
    slope_local = -jnp.stack(
        [
            jnp.sum(self_ds * row_gap[None], axis=(1, 2)),
            jnp.sum(self_ds * col_gap[None], axis=(1, 2)),
        ]
    )
    self_ds_blocks = self_ds_b[None]
    self_p_blocks = self_p_b[None]
    query_blocks = query_heads[None]
    grad_blocks = grad_heads[None]
    self_pair = lax.psum_scatter(
        key_terms(
            self_ds_blocks,
            self_p_blocks,
            query_blocks,
            grad_blocks,
            patch_rows * lax.axis_size("seq"),
        ),
        "seq",
        scatter_dimension=0,
        tiled=True,
    )
    self_dk = self_pair[:, 0]
    self_dv = self_pair[:, 1]
    restored = (
        lax.all_to_all(
            self_dq.reshape(patch_rows, -1).astype(jnp.bfloat16),
            "head",
            split_axis=0,
            concat_axis=1,
            tiled=True,
        ),
        lax.all_to_all(
            self_dk.astype(jnp.bfloat16), "head", split_axis=0, concat_axis=1, tiled=True
        ),
        lax.all_to_all(
            self_dv.astype(jnp.bfloat16), "head", split_axis=0, concat_axis=1, tiled=True
        ),
    )
    slope_grad = lax.psum(slope_local, ("seq", "dp")) / patch_total
    memory_all_keys, memory_all_values = (
        lax.all_gather(memory_keys[0], "seq", axis=0, tiled=True),
        lax.all_gather(memory_values[0], "seq", axis=0, tiled=True),
    )
    memory_all_key_heads = heads_of(memory_all_keys, head_count)
    memory_all_value_heads = heads_of(memory_all_values, head_count)
    text_rows = text_queries.shape[1]
    text_start = lax.axis_index("seq") * text_rows
    text_ids = text_page[0]
    own_text = take_rows(text_ids, text_start, text_rows)
    text_query_heads = heads_of(text_queries[0], head_count)
    text_grad_heads = heads_of(text_cotangent[0], head_count)
    block_count = text_rows // text_rows
    text_query_blocks = text_query_heads.reshape(block_count, text_rows, head_count, -1)
    text_grad_blocks = text_grad_heads.reshape(block_count, text_rows, head_count, -1)

    def cross_block(inputs):
        block_queries, block_grads, block_pages = inputs
        block_bias = jnp.where(
            block_pages[:, None] == whole_layout[0][None, :], 0.0, MASK_FILL
        ).astype(jnp.float32)[None]
        result = query_side(
            block_queries, memory_all_key_heads, memory_all_value_heads, block_grads, block_bias
        )
        return (result[0], result[2], result[3], result[4], result[5])

    cross_out = lax.map(
        cross_block, (text_query_blocks, text_grad_blocks, own_text.reshape(block_count, text_rows))
    )
    text_dq = cross_out[0].reshape(text_rows, -1)
    text_ds_b = cross_out[1]
    text_p_b = cross_out[2]
    memory_pair = lax.psum_scatter(
        key_terms(
            text_ds_b,
            text_p_b,
            text_query_blocks,
            text_grad_blocks,
            patch_rows * lax.axis_size("seq"),
        ),
        "seq",
        scatter_dimension=0,
        tiled=True,
    )
    memory_dk = memory_pair[:, 0]
    memory_dv = memory_pair[:, 1]
    return (
        restored[0][None],
        restored[1][None],
        restored[2][None],
        slope_grad,
        text_dq.astype(jnp.bfloat16)[None],
        memory_dk.astype(jnp.bfloat16)[None],
        memory_dv.astype(jnp.bfloat16)[None],
    )


def solution(mesh):
    in_specs = (
        P("dp", ("seq", "head"), None),
        P("dp", ("seq", "head"), None),
        P("dp", ("seq", "head"), None),
        P("dp", ("seq", "head"), None),
        P("dp", "seq", "head"),
        P("dp", "seq", "head"),
        P("dp", "seq", "head"),
        P("dp", "seq", "head"),
        P(None, "head"),
        P("dp", None),
        P("dp", None),
        P("dp", None),
    )
    out_specs = (
        P("dp", ("seq", "head"), None),
        P("dp", ("seq", "head"), None),
        P("dp", ("seq", "head"), None),
        P(None, "head"),
        P("dp", "seq", "head"),
        P("dp", "seq", "head"),
        P("dp", "seq", "head"),
    )
    return jax.shard_map(local, mesh=mesh, in_specs=in_specs, out_specs=out_specs, check_vma=False)
```

profile of v0, /device:TPU:2, one launch (start us, length us, event | category | flops | bytes accessed | tf_op | source)
XLA Modules:
  0.0 406.0 jit_solution(9305916653580052399)
XLA Ops:
  7.3 1.0 all_to_all.85
  8.3 10.0 %all_to_all.109 = bf16[32,4,640]{2,0,1:T(8,128)(2,1)} all-to-all(bf16[32,4,640]{2,0,1:T(8,128)(2,1)S(1)} %copy.117), channel_id=1, replica_groups=mesh['seq'=16,'head'=4,'dp'=4] {'head'}, dimensions={1} | all-to-all | bytes 327680 | tf_op jit(solution)/shard_map/all_to_all | solution.py:97
  19.4 9.2 %all_to_all.110 = bf16[32,4,640]{2,0,1:T(8,128)(2,1)} all-to-all(bf16[32,4,640]{2,0,1:T(8,128)(2,1)S(1)} %copy.122), channel_id=1, replica_groups=mesh['seq'=16,'head'=4,'dp'=4] {'head'}, dimensions={1} | all-to-all | bytes 327680 | tf_op jit(solution)/shard_map/all_to_all | solution.py:98
  28.6 1.7 copy.136
  30.4 1.0 all_to_all.82
  32.1 4.7 %all-to-all-start = ((bf16[32,4,640]{2,0,1:T(8,128)(2,1)}), bf16[32,4,640]{2,0,1:T(8,128)(2,1)S(1)}, u32[]{:S(2)}, u32[]{:S(2)}) async-start(bf16[32,4,640]{2,0,1:T(8,128)(2,1)} %copy.116), calls=%async_computation | async-start | bytes 327680 | tf_op jit(solution)/shard_map/all_to_all | solution.py:96
  36.8 1.7 copy.140
  41.4 1.8 abs_convert_fusion
  44.2 4.8 %all-to-all-start.2 = ((bf16[32,4,640]{2,0,1:T(8,128)(2,1)}), bf16[32,4,640]{2,0,1:T(8,128)(2,1)S(1)}, u32[]{:S(2)}, u32[]{:S(2)}) async-start(bf16[32,4,640]{2,0,1:T(8,128)(2,1)} %copy.121), calls=%async_computation.2 | async-start | bytes 327680 | tf_op jit(solution)/shard_map/all_to_all | solution.py:99
  49.4 4.3 %all-to-all-done.2 = bf16[32,4,640]{2,0,1:T(8,128)(2,1)S(1)} async-done(((bf16[32,4,640]{2,0,1:T(8,128)(2,1)}), bf16[32,4,640]{2,0,1:T(8,128)(2,1)S(1)}, u32[]{:S(2)}, u32[]{:S(2)}) %all-to-all-start.2) | async-done | bytes 163872 | tf_op jit(solution)/shard_map/all_to_all | solution.py:99
  54.1 6.2 %all-gather.7.cloned.1.call-done = bf16[2048,640]{1,0:T(8,128)(2,1)} async-done(((bf16[128,640]{1,0:T(8,128)(2,1)}), bf16[2048,640]{1,0:T(8,128)(2,1)}) %all-gather.7.cloned.1.call-update) | async-done | bytes 2621456 | tf_op jit(solution)/shard_map/all_gather | solution.py:104
  60.3 3.0 copy.118
  63.3 37.8 %all-gather.9.cloned.1.call-done = bf16[2048,640]{1,0:T(8,128)(2,1)} async-done(((bf16[128,640]{1,0:T(8,128)(2,1)}), bf16[2048,640]{1,0:T(8,128)(2,1)}) %all-gather.9.cloned.1.call-update) | async-done | bytes 2621456 | tf_op jit(solution)/shard_map/all_gather | solution.py:105
  101.0 4.5 %copy.123 = bf16[2048,640]{0,1:T(8,128)(2,1)} copy(bf16[2048,640]{1,0:T(8,128)(2,1)} %all-gather.9.cloned.1.call-done) | data formatting | bytes 5242880 | tf_op jit(solution)/shard_map/all_gather | solution.py:105
  105.5 3.6 select_add_fusion
  109.1 1.6 fusion.28
  110.7 1.0 copy-done.4
  111.7 1.0 copy-done.7
  112.7 1.3 multiply_reduce_fusion.3
  114.3 2.4 multiply_reduce_fusion.2
  116.7 3.2 convolution_multiply_fusion
  119.8 6.0 %copy.131 = f32[2048,1,640]{2,0,1:T(8,128)} copy(f32[2048,1,640]{0,2,1:T(8,128)} %bitcast.79) | data formatting | bytes 10485760 | tf_op jit(solution)/shard_map/stack;reshape | solution.py:77
  125.8 8.0 %fusion.7 = f32[5,2048,128]{1,2,0:T(8,128)} fusion(bf16[128,5,128]{0,2,1:T(8,128)(2,1)S(1)} %copy.130, f32[5,128]{1,0:T(8,128)S(1)} %get-tuple-element.85, f32[5,128,2048]{2,1,0:T(8,128)} %copy-done.4), kind=kOutput, calls=%fused_computation.22 | convolution fusion | flops 339479168 | bytes 10652160 | tf_op jit(solution)/shard_map/chrk,crhs->khs/dot_general | solution.py:74
  133.7 5.9 %copy.132 = f32[2048,1,640]{2,0,1:T(8,128)} copy(f32[2048,1,640]{0,2,1:T(8,128)} %bitcast.84) | data formatting | bytes 10485760 | tf_op jit(solution)/shard_map/stack;reshape | solution.py:77
  139.6 8.8 %pad_maximum_fusion = f32[2048,2,640]{2,0,1:T(8,128)} fusion(f32[2048,1,640]{2,0,1:T(8,128)} %copy.132, f32[2048,1,640]{2,0,1:T(8,128)} %copy.131), kind=kLoop, calls=%fused_computation.2 | loop fusion | flops 2621440 | bytes 20971520 | tf_op jit(solution)/shard_map/stack | solution.py:77
  149.6 1.1 copy.139
  150.8 1.6 compare_select_fusion
  152.4 9.5 %fusion.29 = (f32[5,256]{1,0:T(8,128)S(1)}, f32[5,256,2048]{2,1,0:T(8,128)}) fusion(f32[256,2048]{1,0:T(8,128)} %compare_select_fusion, bf16[256,5,128]{0,2,1:T(8,128)(2,1)S(1)} %bitcast.87, bf16[2048,5,128]{0,2,1:T(8,128)(2,1)} %bitcast.104), kind=kOutput, calls=%fused_computation.62 | convolution fusion | flops 681576448 | bytes 15537152 | tf_op jit(solution)/shard_map/while/body/eval_jaxpr/sub | solution.py:44
  161.8 27.1 %all-gather.13.cloned.1.call-done = bf16[1,2048,640]{1,2,0:T(8,128)(2,1)} async-done(((bf16[1,128,640]{1,2,0:T(8,128)(2,1)}), bf16[1,2048,640]{1,2,0:T(8,128)(2,1)}) %all-gather.13.cloned.1.call-update) | async-done | bytes 2621456 | tf_op jit(solution)/shard_map/all_gather | solution.py:163
  189.0 6.1 %multiply_reduce_fusion = (f32[5,256]{1,0:T(8,128)S(1)}, f32[5,256,2048]{2,1,0:T(8,128)S(1)}) fusion(f32[5,256,2048]{2,1,0:T(8,128)} %get-tuple-element.90, f32[5,256]{1,0:T(8,128)S(1)} %get-tuple-element.89, bf16[256,5,128]{0,2,1:T(8,128)(2,1)S(1)} %bitcast.96, bf16[2048,5,128]{0,2,1:T(8,128)(2,1)} %bitcast.106), kind=kOutput, calls=%fused_computation.5 | convolution fusion | flops 678951680 | bytes 23930880 | tf_op jit(solution)/shard_map/while/body/eval_jaxpr/rhs,khs->hrk/dot_general | solution.py:48
  195.1 1.1 slice-done.1
  196.8 1.8 multiply_convert_fusion
  198.6 3.9 convolution_multiply_fusion.1
  202.6 5.9 %copy.143 = f32[2048,1,640]{2,0,1:T(8,128)} copy(f32[2048,1,640]{0,2,1:T(8,128)} %bitcast.78) | data formatting | bytes 10485760 | tf_op jit(solution)/shard_map/stack;reshape | solution.py:77
  208.5 7.4 %fusion.3 = f32[5,2048,128]{1,2,0:T(8,128)} fusion(bf16[256,5,128]{0,2,1:T(8,128)(2,1)S(1)} %bitcast.97, f32[5,256,2048]{2,1,0:T(8,128)} %get-tuple-element.90, f32[5,256]{1,0:T(8,128)S(1)} %get-tuple-element.89), kind=kOutput, calls=%fused_computation.9 | convolution fusion | flops 676331520 | bytes 16061440 | tf_op jit(solution)/shard_map/chrk,crhs->khs/dot_general | solution.py:74
  215.9 5.9 %copy.144 = f32[2048,1,640]{2,0,1:T(8,128)} copy(f32[2048,1,640]{0,2,1:T(8,128)} %bitcast.85) | data formatting | bytes 10485760 | tf_op jit(solution)/shard_map/stack;reshape | solution.py:77
  221.9 8.7 %pad_maximum_fusion.1 = f32[2048,2,640]{2,0,1:T(8,128)} fusion(f32[2048,1,640]{2,0,1:T(8,128)} %copy.144, f32[2048,1,640]{2,0,1:T(8,128)} %copy.143), kind=kLoop, calls=%fused_computation.3 | loop fusion | flops 2621440 | bytes 20971520 | tf_op jit(solution)/shard_map/stack | solution.py:77
  230.6 5.3 %fusion.14 = bf16[5,256,128]{1,2,0:T(8,128)(2,1)S(1)} fusion(bf16[5,256,2048]{2,1,0:T(8,128)(2,1)} %copy-done.2, bf16[2048,5,128]{0,2,1:T(8,128)(2,1)} %bitcast.105), kind=kOutput, calls=%fused_computation.31 | convolution fusion | flops 671416320 | bytes 8192000 | tf_op jit(solution)/shard_map/while/body/eval_jaxpr/hrk,khs->rhs/dot_general | solution.py:55
  236.9 129.5 %psum.7 = f32[2,5]{1,0:T(2,128)S(1)} all-reduce(f32[2,5]{1,0:T(2,128)S(1)} %maximum_negate_fusion), channel_id=1, replica_groups=mesh['seq'=16,'head'=4,'dp'=4] {'seq','dp'}, use_global_device_ids=true, to_apply=%region_10.11 | all-reduce | flops 10 | bytes 80 | tf_op jit(solution)/shard_map/psum | solution.py:160
  366.3 2.6 fusion.21
  369.9 4.8 %all-to-all-start.4 = ((bf16[4,32,640]{2,1,0:T(8,128)(2,1)}), bf16[4,32,640]{2,1,0:T(8,128)(2,1)S(1)}, u32[]{:S(2)}, u32[]{:S(2)}) async-start(bf16[4,32,640]{2,1,0:T(8,128)(2,1)} %convert_element_type.95), calls=%async_computation.4 | async-start | bytes 327680 | tf_op jit(solution)/shard_map/all_to_all | solution.py:146
  374.7 1.1 convert.8
  376.6 2.8 all-to-all-done.4
  379.4 4.8 %all-to-all-start.5 = ((bf16[4,32,640]{2,1,0:T(8,128)(2,1)}), bf16[4,32,640]{2,1,0:T(8,128)(2,1)S(1)}, u32[]{:S(2)}, u32[]{:S(2)}) async-start(bf16[4,32,640]{2,1,0:T(8,128)(2,1)} %bitcast.21), calls=%async_computation.6 | async-start | bytes 327680 | tf_op jit(solution)/shard_map/all_to_all | solution.py:153
  385.6 1.1 convert.9
  386.7 2.2 all-to-all-done.5
  388.9 4.8 %all-to-all-start.6 = ((bf16[4,32,640]{2,1,0:T(8,128)(2,1)}), bf16[4,32,640]{2,1,0:T(8,128)(2,1)S(1)}, u32[]{:S(2)}, u32[]{:S(2)}) async-start(bf16[4,32,640]{2,1,0:T(8,128)(2,1)} %bitcast.23), calls=%async_computation.7 | async-start | bytes 327680 | tf_op jit(solution)/shard_map/all_to_all | solution.py:156
  395.2 3.1 all-to-all-done.6
  (77 shorter events, 15.1 us)
Async XLA Ops:
  7.2 143.6 %copy-start = (s32[1,4096]{1,0:T(1,128)S(1)}, s32[1,4096]{1,0:T(1,128)}, u32[]{:S(2)}) copy-start(s32[1,4096]{1,0:T(1,128)} %param.23) | copy-start | bytes 49156
  7.2 36.3 %copy-start.9 = (bf16[1,32,2560]{2,1,0:T(8,128)(2,1)S(1)}, bf16[1,32,2560]{2,1,0:T(8,128)(2,1)}, u32[]{:S(2)}) copy-start(bf16[1,32,2560]{2,1,0:T(8,128)(2,1)} %param.15) | copy-start | bytes 491524
  7.2 41.8 %copy-start.10 = (f32[2,5]{1,0:T(2,128)S(1)}, f32[2,5]{1,0:T(2,128)}, u32[]{:S(2)}) copy-start(f32[2,5]{1,0:T(2,128)} %param.20) | copy-start | bytes 124
  7.2 53.1 %all-gather.7.cloned.1.call-start = ((), (), s32[]{:S(2)}) async-start(), calls=%async_computation.9 | async-start | bytes 2785280 | tf_op jit(solution)/shard_map/all_gather | solution.py:104
  18.3 82.7 %all-gather.9.cloned.1.call-start = ((), (), s32[]{:S(2)}) async-start(), calls=%async_computation.10 | async-start | bytes 2785280 | tf_op jit(solution)/shard_map/all_gather | solution.py:105
  28.6 123.8 %all-gather.11.cloned.1.call-start = ((), (), s32[]{:S(2)}) async-start(), calls=%async_computation.13 | async-start | bytes 2785280 | tf_op jit(solution)/shard_map/all_gather | solution.py:162
  32.1 12.1 %all-to-all-start = ((bf16[32,4,640]{2,0,1:T(8,128)(2,1)}), bf16[32,4,640]{2,0,1:T(8,128)(2,1)S(1)}, u32[]{:S(2)}, u32[]{:S(2)}) async-start(bf16[32,4,640]{2,0,1:T(8,128)(2,1)} %copy.116), calls=%async_computation | async-start | bytes 327680 | tf_op jit(solution)/shard_map/all_to_all | solution.py:96
  36.8 152.2 %all-gather.13.cloned.1.call-start = ((), (), s32[]{:S(2)}) async-start(), calls=%async_computation.14 | async-start | bytes 2785280 | tf_op jit(solution)/shard_map/all_gather | solution.py:163
  44.2 9.5 %all-to-all-start.2 = ((bf16[32,4,640]{2,0,1:T(8,128)(2,1)}), bf16[32,4,640]{2,0,1:T(8,128)(2,1)S(1)}, u32[]{:S(2)}, u32[]{:S(2)}) async-start(bf16[32,4,640]{2,0,1:T(8,128)(2,1)} %copy.121), calls=%async_computation.2 | async-start | bytes 327680 | tf_op jit(solution)/shard_map/all_to_all | solution.py:99
  49.0 325.7 %reduce-scatter.3.cloned.1.call-start = ((), (), s32[]{:S(2)}) async-start(), calls=%async_computation.11 | async-start | bytes 11141120 | tf_op jit(solution)/shard_map/reduce_scatter | solution.py:131
  63.3 45.8 %copy-start.3 = (bf16[2048,640]{0,1:T(8,128)(2,1)}, bf16[2048,640]{0,1:T(8,128)(2,1)S(1)}, u32[]{:S(2)}) copy-start(bf16[2048,640]{0,1:T(8,128)(2,1)S(1)} %copy.118) | copy-start | bytes 7864324
  109.1 2.7 copy-start.4
  109.1 3.6 copy-start.7
  112.7 1.3 copy-start.5
  112.7 1.6 copy-start.6
  148.4 1.0 copy-start.8
  148.5 237.1 %reduce-scatter.5.cloned.1.call-start = ((), (), s32[]{:S(2)}) async-start(), calls=%async_computation.12 | async-start | bytes 11141120 | tf_op jit(solution)/shard_map/reduce_scatter | solution.py:193
  189.0 6.1 %slice-start = ((s8[10485760]{0:T(1024)(128)(4,1)}), s8[4194304]{0:T(1024)(128)(4,1)S(1)}, s32[]{:S(2)}) async-start(s8[10485760]{0:T(1024)(128)(4,1)} %bitcast.80), calls=%async_computation.15 | async-start | bytes 8388608
  189.0 7.3 %slice-start.1 = ((s8[10485760]{0:T(1024)(128)(4,1)}), s8[4194304]{0:T(1024)(128)(4,1)S(1)}, s32[]{:S(2)}) async-start(s8[10485760]{0:T(1024)(128)(4,1)} %bitcast.80), calls=%async_computation.16 | async-start | bytes 8388608
  189.0 7.9 %slice-start.2 = ((s8[10485760]{0:T(1024)(128)(4,1)}), s8[2097152]{0:T(1024)(128)(4,1)S(1)}, s32[]{:S(2)}) async-start(s8[10485760]{0:T(1024)(128)(4,1)} %bitcast.80), calls=%async_computation.17 | async-start | bytes 4194304
  198.6 4.0 copy-start.2
  236.9 162.3 %copy-start.1 = (s32[1,4096]{1,0:T(1,128)S(1)}, s32[1,4096]{1,0:T(1,128)}, u32[]{:S(2)}) copy-start(s32[1,4096]{1,0:T(1,128)} %param.23) | copy-start | bytes 49156
  369.9 9.5 %all-to-all-start.4 = ((bf16[4,32,640]{2,1,0:T(8,128)(2,1)}), bf16[4,32,640]{2,1,0:T(8,128)(2,1)S(1)}, u32[]{:S(2)}, u32[]{:S(2)}) async-start(bf16[4,32,640]{2,1,0:T(8,128)(2,1)} %convert_element_type.95), calls=%async_computation.4 | async-start | bytes 327680 | tf_op jit(solution)/shard_map/all_to_all | solution.py:146
  379.4 9.5 %all-to-all-start.5 = ((bf16[4,32,640]{2,1,0:T(8,128)(2,1)}), bf16[4,32,640]{2,1,0:T(8,128)(2,1)S(1)}, u32[]{:S(2)}, u32[]{:S(2)}) async-start(bf16[4,32,640]{2,1,0:T(8,128)(2,1)} %bitcast.21), calls=%async_computation.6 | async-start | bytes 327680 | tf_op jit(solution)/shard_map/all_to_all | solution.py:153
  388.9 9.5 %all-to-all-start.6 = ((bf16[4,32,640]{2,1,0:T(8,128)(2,1)}), bf16[4,32,640]{2,1,0:T(8,128)(2,1)S(1)}, u32[]{:S(2)}, u32[]{:S(2)}) async-start(bf16[4,32,640]{2,1,0:T(8,128)(2,1)} %bitcast.23), calls=%async_computation.7 | async-start | bytes 327680 | tf_op jit(solution)/shard_map/all_to_all | solution.py:156
Sparse Core Ops, SparseCore 0:
  18.5 41.7 all-gather.6
  62.1 38.8 all-gather.8
  103.4 41.4 all-gather.10
  147.0 41.9 all-gather.12
  191.4 73.8 reduce-scatter.2
  267.7 74.0 reduce-scatter.4
where the time goes:
time: 408 us; the launch traced here: 406 us
  blocking collectives  149 us (37%)
  waiting for transfers between devices  83.5 us (20%)
  local copies, waits for them, and re-layouts  52.1 us (13%)
  matrix products  50.7 us (12%)
  other arithmetic  32.3 us (8%)
  starting transfers between devices  24.2 us (6%)
  between operations  14.4 us (4%)
    psum x1, blocking collectives, local(): slope_grad = lax.psum(slope_local, ('seq', 'dp')) / patch_total  129 us
    all_gather x1, waiting for transfers between devices, local(): lax.all_gather(local_values, 'seq', axis=0, tiled=True)  37.8 us
    all_gather x1, waiting for transfers between devices, local(): lax.all_gather(memory_values[0], 'seq', axis=0, tiled=True)  27.1 us
    another operation x4, local copies, waits for them, and re-layouts, key_terms(): jnp.stack([key_grad.reshape(row_count, -1), value_grad.reshape(row_count,...  23.7 us
    another operation x2, other arithmetic, key_terms(): jnp.stack([key_grad.reshape(row_count, -1), value_grad.reshape(row_count,...  17.5 us
    dot_general x2, matrix products, key_terms(): jnp.einsum('chrk,crhs->khs', softmax_b, grad_rows, preferred_element_type...  15.4 us
    unnamed x33, local copies, waits for them, and re-layouts  10.6 us
    all_to_all x1, blocking collectives, local(): lax.all_to_all(self_keys[0], 'head', split_axis=1, concat_axis=0, tiled=T...  10 us
  transfers between devices with their start and end apart: 11, of which 7 were waited for; matrix products, arithmetic and copies ran while one was open for 31% of the time, Pallas kernels for 0%

commit v1 on v0

--- a/solution.py
+++ b/solution.py
@@ -1,9 +1,39 @@
+import functools
 import jax
 import jax.numpy as jnp
 from jax import lax
 from jax.sharding import PartitionSpec as P
 
 MASK_FILL = -1e30
+
+
+def build_chains(x0, net_axis, pos_dim):
+    z2 = lax.psum(1, net_axis)
+    right_arr, view_out, y_new = (z2, lax.axis_index(net_axis), x0.shape[pos_dim])
+    fields = [(k0, (k0 + 1) % right_arr) for k0 in range(right_arr)]
+    block_out = jnp.zeros(
+        (*x0.shape[:pos_dim], right_arr * y_new, *x0.shape[pos_dim + 1 :]), x0.dtype
+    )
+    block_out = lax.dynamic_update_slice_in_dim(block_out, x0, view_out * y_new, axis=pos_dim)
+    w_next = block_now = x0
+    store = [(k0, (k0 - 1) % right_arr) for k0 in range(right_arr)]
+    nth = 1
+    piece_out = right_arr // 2
+    while nth < piece_out + 1:
+        w_next = lax.ppermute(w_next, net_axis, fields)
+        block_out = lax.dynamic_update_slice_in_dim(
+            block_out, w_next, (view_out - nth) % right_arr * y_new, axis=pos_dim
+        )
+        if nth < right_arr - piece_out:
+            block_now = lax.ppermute(block_now, net_axis, store)
+            block_out = lax.dynamic_update_slice_in_dim(
+                block_out, block_now, (view_out + nth) % right_arr * y_new, axis=pos_dim
+            )
+        nth += 1
+    return block_out
+
+
+shape_loops = functools.partial(build_chains, net_axis="seq", pos_dim=0)
 
 
 def page_layout(counts, widths, patch_total):
@@ -102,7 +132,7 @@
     patch_rows = local_queries.shape[0]
     all_keys, all_values = (
         lax.all_gather(local_keys, "seq", axis=0, tiled=True),
-        lax.all_gather(local_values, "seq", axis=0, tiled=True),
+        shape_loops(local_values),
     )
     patch_total = all_keys.shape[0]
     whole_layout = page_layout(page_counts[0], page_cols[0], patch_total)

time: 408 us -> 387 us (0.949)
  waiting for transfers between devices: 83.5 us -> 30.2 us
  starting transfers between devices: 24.2 us -> 51.2 us
  blocking collectives: 149 us -> 137 us
  local copies, waits for them, and re-layouts: 52.1 us -> 60.6 us
  other arithmetic: 32.3 us -> 36.8 us
    all_gather x1 -> x0, waiting for transfers between devices: 37.8 us -> none  [local(): lax.all_gather(local_values, 'seq', axis=0, tiled=True)]
    all_gather x1, waiting for transfers between devices: 27.1 us -> 0.01 us  [local(): lax.all_gather(memory_values[0], 'seq', axis=0, tiled=True)]
    ppermute x0 -> x15, starting transfers between devices: none -> 20.3 us  [the longest x7 20.2 us: build_chains(): block_now = lax.ppermute(block_now, net_axis, store)]
    ppermute x0 -> x15, waiting for transfers between devices: none -> 18.9 us  [the longest x7 10.6 us: build_chains(): block_now = lax.ppermute(block_now, net_axis, store)]
    ppermute x0 -> x15, local copies, waits for them, and re-layouts: none -> 11.6 us  [the longest x7 6.6 us: build_chains(): block_now = lax.ppermute(block_now, net_axis, store)]
    all_to_all x1 -> x0, blocking collectives: 9.2 us -> none  [local(): lax.all_to_all(self_values[0], 'head', split_axis=1, concat_axis=0, tiled...]
    all_gather x1, waiting for transfers between devices: 6.16 us -> 0.01 us  [local(): lax.all_gather(local_keys, 'seq', axis=0, tiled=True)]
    all_to_all x0 -> x1, starting transfers between devices: none -> 4.77 us  [local(): lax.all_to_all(self_values[0], 'head', split_axis=1, concat_axis=0, tiled...]
  transfers between devices with their start and end apart: 11 -> 26, of which waited for: 7 -> 17; matrix products, arithmetic and copies ran while one was open for 31% -> 38% of each run, Pallas kernels for 0% -> 0%
where the time goes in v1:
time: 387 us; the launch traced here: 385 us
  blocking collectives  137 us (35%)
  local copies, waits for them, and re-layouts  60.6 us (16%)
  matrix products  54.5 us (14%)
  starting transfers between devices  51.2 us (13%)
  other arithmetic  36.8 us (10%)
  waiting for transfers between devices  30.2 us (8%)
  between operations  14.3 us (4%)
    psum x1, blocking collectives, local(): slope_grad = lax.psum(slope_local, ('seq', 'dp')) / patch_total  127 us
    another operation x4, local copies, waits for them, and re-layouts, key_terms(): jnp.stack([key_grad.reshape(row_count, -1), value_grad.reshape(row_count,...  23.8 us
    ppermute x7, starting transfers between devices, build_chains(): block_now = lax.ppermute(block_now, net_axis, store)  20.2 us
    another operation x2, other arithmetic, key_terms(): jnp.stack([key_grad.reshape(row_count, -1), value_grad.reshape(row_count,...  17.6 us
    dot_general x2, matrix products, key_terms(): jnp.einsum('chrk,crhs->khs', softmax_b, grad_rows, preferred_element_type...  15.5 us
    ppermute x7, waiting for transfers between devices, build_chains(): block_now = lax.ppermute(block_now, net_axis, store)  10.6 us
    unnamed x47, local copies, waits for them, and re-layouts  10.2 us
    dot_general x2, matrix products, query_side(): jnp.einsum('rhs,khs->hrk', grad_rows, value_rows, preferred_element_type=...  10 us
  transfers between devices with their start and end apart: 26, of which 17 were waited for; matrix products, arithmetic and copies ran while one was open for 38% of the time, Pallas kernels for 0%

profile of v1, /device:TPU:2, one launch (start us, length us, event | category | flops | bytes accessed | tf_op | source)
XLA Modules:
  0.0 385.1 jit_solution(2022847882685469063)
XLA Ops:
  8.4 10.0 %all_to_all.109 = bf16[32,4,640]{2,0,1:T(8,128)(2,1)} all-to-all(bf16[32,4,640]{2,0,1:T(8,128)(2,1)S(1)} %copy.166), channel_id=1, replica_groups=mesh['seq'=16,'head'=4,'dp'=4] {'head'}, dimensions={1} | all-to-all | bytes 327680 | tf_op jit(solution)/shard_map/all_to_all | solution.py:127
  18.4 1.7 copy.201
  21.8 4.8 %all-to-all-start.2 = ((bf16[32,4,640]{2,0,1:T(8,128)(2,1)}), bf16[32,4,640]{2,0,1:T(8,128)(2,1)S(1)}, u32[]{:S(2)}, u32[]{:S(2)}) async-start(bf16[32,4,640]{2,0,1:T(8,128)(2,1)} %copy.170), calls=%async_computation.2 | async-start | bytes 327680 | tf_op jit(solution)/shard_map/all_to_all | solution.py:128
  26.6 1.7 copy.205
  31.2 1.7 abs_convert_fusion
  34.6 4.8 %all-to-all-start = ((bf16[32,4,640]{2,0,1:T(8,128)(2,1)}), bf16[32,4,640]{2,0,1:T(8,128)(2,1)S(1)}, u32[]{:S(2)}, u32[]{:S(2)}) async-start(bf16[32,4,640]{2,0,1:T(8,128)(2,1)} %copy.165), calls=%async_computation | async-start | bytes 327680 | tf_op jit(solution)/shard_map/all_to_all | solution.py:126
  40.7 3.4 all-to-all-done
  44.1 4.8 %all-to-all-start.3 = ((bf16[32,4,640]{2,0,1:T(8,128)(2,1)}), bf16[32,4,640]{2,0,1:T(8,128)(2,1)S(1)}, u32[]{:S(2)}, u32[]{:S(2)}) async-start(bf16[32,4,640]{2,0,1:T(8,128)(2,1)} %copy.187), calls=%async_computation.3 | async-start | bytes 327680 | tf_op jit(solution)/shard_map/all_to_all | solution.py:129
  51.1 2.4 all-to-all-done.3
  55.5 3.2 collective-permute-start.3
  58.8 1.6 collective-permute-done.2
  62.0 3.0 collective-permute-start.5
  65.1 2.5 collective-permute-done.4
  69.0 3.2 collective-permute-start.7
  72.3 1.6 collective-permute-done.6
  77.4 3.2 collective-permute-start.9
  82.0 1.7 collective-permute-done.9
  84.8 3.1 collective-permute-start.11
  90.1 2.6 collective-permute-done.11
  93.8 3.1 collective-permute-start.13
  97.3 4.5 %collective-permute-done.13 = bf16[128,640]{1,0:T(8,128)(2,1)} collective-permute-done((bf16[128,640]{1,0:T(8,128)(2,1)}, bf16[128,640]{1,0:T(8,128)(2,1)}, u32[]{:S(2)}, u32[]{:S(2)}) %collective-permute-start.13) | collective-permute-done | bytes 163872 | tf_op jit(solution)/shard_map/ppermute | solution.py:28
  106.0 3.0 copy.167
  109.0 4.5 %select_add_fusion = f32[5,128,2048]{2,1,0:T(8,128)S(1)} fusion(bf16[128,5,128]{0,2,1:T(8,128)(2,1)S(1)} %copy.194, bf16[2048,5,128]{0,2,1:T(8,128)(2,1)S(1)} %bitcast.90, f32[128,2048]{1,0:T(8,128)} %get-tuple-element.93, f32[5]{0:T(128)S(1)} %copy-done.17, f32[128,2048]{1,0:T(8,128)} %get-tuple-element.94, f32[5]{0:T(128)S(1)} %copy-done.16, ...), kind=kOutput, calls=%fused_computation.21 | convolution fusion | flops 344719360 | bytes 10387496 | tf_op jit(solution)/shard_map/rhs,khs->hrk/dot_general | solution.py:70
  113.6 3.7 fusion.31
  117.5 7.9 %fusion.9 = f32[5,2048,128]{1,2,0:T(8,128)} fusion(bf16[128,5,128]{0,2,1:T(8,128)(2,1)S(1)} %copy.195, f32[5,128]{1,0:T(8,128)S(1)} %get-tuple-element.85, f32[5,128,2048]{2,1,0:T(8,128)} %copy-done.4), kind=kOutput, calls=%fused_computation.24 | convolution fusion | flops 339479168 | bytes 10652160 | tf_op jit(solution)/shard_map/chrk,crhs->khs/dot_general | solution.py:104
  125.4 6.1 %copy.197 = f32[2048,1,640]{2,0,1:T(8,128)} copy(f32[2048,1,640]{0,2,1:T(8,128)} %bitcast.92) | data formatting | bytes 10485760 | tf_op jit(solution)/shard_map/stack;reshape | solution.py:107
  131.4 3.8 fusion.3
  135.2 4.2 %multiply_reduce_fusion.2 = (f32[5]{0:T(128)S(1)}, f32[5]{0:T(128)S(1)}, bf16[5,128,2048]{2,1,0:T(8,128)(2,1)S(1)}) fusion(f32[128,2048]{1,0:T(8,128)S(1)} %copy-done.6, f32[128,2048]{1,0:T(8,128)S(1)} %copy-done.5, f32[5,128]{1,0:T(8,128)S(1)} %get-tuple-element.87, f32[5,2048,128]{1,2,0:T(8,128)S(1)} %get-tuple-element.88, ...), kind=kLoop, calls=%fused_computation.19 | loop fusion | flops 10485750 | bytes 15209512 | tf_op jit(solution)/shard_map/reduce_sum | solution.py:153
  139.4 3.2 convolution_multiply_fusion
  142.5 5.9 %copy.196 = f32[2048,1,640]{2,0,1:T(8,128)} copy(f32[2048,1,640]{0,2,1:T(8,128)} %bitcast.87) | data formatting | bytes 10485760 | tf_op jit(solution)/shard_map/stack;reshape | solution.py:107
  148.4 8.8 %pad_maximum_fusion = f32[2048,2,640]{2,0,1:T(8,128)} fusion(f32[2048,1,640]{2,0,1:T(8,128)} %copy.197, f32[2048,1,640]{2,0,1:T(8,128)} %copy.196), kind=kLoop, calls=%fused_computation.2 | loop fusion | flops 2621440 | bytes 20971520 | tf_op jit(solution)/shard_map/stack | solution.py:107
  159.6 1.5 compare_select_fusion
  161.1 9.5 %fusion.32 = (f32[5,256]{1,0:T(8,128)S(1)}, f32[5,256,2048]{2,1,0:T(8,128)}) fusion(f32[256,2048]{1,0:T(8,128)} %compare_select_fusion, bf16[256,5,128]{0,2,1:T(8,128)(2,1)S(1)} %bitcast.95, bf16[2048,5,128]{0,2,1:T(8,128)(2,1)} %bitcast.114), kind=kOutput, calls=%fused_computation.80 | convolution fusion | flops 681576448 | bytes 15537152 | tf_op jit(solution)/shard_map/while/body/eval_jaxpr/sub | solution.py:74
  170.6 7.7 %fusion.5 = f32[5,2048,128]{1,2,0:T(8,128)} fusion(bf16[256,5,128]{0,2,1:T(8,128)(2,1)S(1)} %bitcast.106, f32[5,256,2048]{2,1,0:T(8,128)} %get-tuple-element.90, f32[5,256]{1,0:T(8,128)S(1)} %get-tuple-element.89), kind=kOutput, calls=%fused_computation.13 | convolution fusion | flops 676331520 | bytes 16061440 | tf_op jit(solution)/shard_map/chrk,crhs->khs/dot_general | solution.py:104
  178.2 5.9 %copy.209 = f32[2048,1,640]{2,0,1:T(8,128)} copy(f32[2048,1,640]{0,2,1:T(8,128)} %bitcast.93) | data formatting | bytes 10485760 | tf_op jit(solution)/shard_map/stack;reshape | solution.py:107
  184.2 6.3 %multiply_reduce_fusion = (f32[5,256]{1,0:T(8,128)S(1)}, f32[5,256,2048]{2,1,0:T(8,128)S(1)}) fusion(f32[5,256,2048]{2,1,0:T(8,128)} %get-tuple-element.90, f32[5,256]{1,0:T(8,128)S(1)} %get-tuple-element.89, bf16[256,5,128]{0,2,1:T(8,128)(2,1)S(1)} %bitcast.107, bf16[2048,5,128]{0,2,1:T(8,128)(2,1)} %bitcast.116), kind=kOutput, calls=%fused_computation.5 | convolution fusion | flops 678951680 | bytes 23930880 | tf_op jit(solution)/shard_map/while/body/eval_jaxpr/rhs,khs->hrk/dot_general | solution.py:78
  192.4 1.8 multiply_convert_fusion
  194.2 3.8 convolution_multiply_fusion.1
  198.1 6.0 %copy.208 = f32[2048,1,640]{2,0,1:T(8,128)} copy(f32[2048,1,640]{0,2,1:T(8,128)} %bitcast.86) | data formatting | bytes 10485760 | tf_op jit(solution)/shard_map/stack;reshape | solution.py:107
  204.1 8.8 %pad_maximum_fusion.1 = f32[2048,2,640]{2,0,1:T(8,128)} fusion(f32[2048,1,640]{2,0,1:T(8,128)} %copy.209, f32[2048,1,640]{2,0,1:T(8,128)} %copy.208), kind=kLoop, calls=%fused_computation.3 | loop fusion | flops 2621440 | bytes 20971520 | tf_op jit(solution)/shard_map/stack | solution.py:107
  212.9 5.3 %fusion.16 = bf16[5,256,128]{1,2,0:T(8,128)(2,1)S(1)} fusion(bf16[5,256,2048]{2,1,0:T(8,128)(2,1)} %copy-done.2, bf16[2048,5,128]{0,2,1:T(8,128)(2,1)} %bitcast.115), kind=kOutput, calls=%fused_computation.33 | convolution fusion | flops 671416320 | bytes 8192000 | tf_op jit(solution)/shard_map/while/body/eval_jaxpr/hrk,khs->rhs/dot_general | solution.py:85
  219.1 2.6 fusion.23
  222.8 6.8 %all-to-all-start.4 = ((bf16[4,32,640]{2,1,0:T(8,128)(2,1)}), bf16[4,32,640]{2,1,0:T(8,128)(2,1)S(1)}, u32[]{:S(2)}, u32[]{:S(2)}) async-start(bf16[4,32,640]{2,1,0:T(8,128)(2,1)} %convert_element_type.95), calls=%async_computation.4 | async-start | bytes 327680 | tf_op jit(solution)/shard_map/all_to_all | solution.py:176
  229.6 127.5 %psum.7 = f32[2,5]{1,0:T(2,128)S(1)} all-reduce(f32[2,5]{1,0:T(2,128)S(1)} %maximum_negate_fusion), channel_id=1, replica_groups=mesh['seq'=16,'head'=4,'dp'=4] {'seq','dp'}, use_global_device_ids=true, to_apply=%region_10.11 | all-reduce | flops 10 | bytes 80 | tf_op jit(solution)/shard_map/psum | solution.py:190
  358.9 4.7 %all-to-all-start.5 = ((bf16[4,32,640]{2,1,0:T(8,128)(2,1)}), bf16[4,32,640]{2,1,0:T(8,128)(2,1)S(1)}, u32[]{:S(2)}, u32[]{:S(2)}) async-start(bf16[4,32,640]{2,1,0:T(8,128)(2,1)} %bitcast.23), calls=%async_computation.6 | async-start | bytes 327680 | tf_op jit(solution)/shard_map/all_to_all | solution.py:183
  366.1 2.2 all-to-all-done.5
  368.3 4.8 %all-to-all-start.6 = ((bf16[4,32,640]{2,1,0:T(8,128)(2,1)}), bf16[4,32,640]{2,1,0:T(8,128)(2,1)S(1)}, u32[]{:S(2)}, u32[]{:S(2)}) async-start(bf16[4,32,640]{2,1,0:T(8,128)(2,1)} %bitcast.25), calls=%async_computation.7 | async-start | bytes 327680 | tf_op jit(solution)/shard_map/all_to_all | solution.py:186
  374.6 3.1 all-to-all-done.6
  (151 shorter events, 42.8 us)
Async XLA Ops:
  7.2 152.4 %copy-start = (s32[1,4096]{1,0:T(1,128)S(1)}, s32[1,4096]{1,0:T(1,128)}, u32[]{:S(2)}) copy-start(s32[1,4096]{1,0:T(1,128)} %param.23) | copy-start | bytes 49156
  7.2 26.6 %copy-start.11 = (bf16[1,32,2560]{2,1,0:T(8,128)(2,1)S(1)}, bf16[1,32,2560]{2,1,0:T(8,128)(2,1)}, u32[]{:S(2)}) copy-start(bf16[1,32,2560]{2,1,0:T(8,128)(2,1)} %param.12) | copy-start | bytes 491524
  7.2 32.2 %copy-start.15 = (f32[2,5]{1,0:T(2,128)S(1)}, f32[2,5]{1,0:T(2,128)}, u32[]{:S(2)}) copy-start(f32[2,5]{1,0:T(2,128)} %param.20) | copy-start | bytes 124
  7.2 32.7 %copy-start.12 = (bf16[1,32,2560]{2,1,0:T(8,128)(2,1)S(1)}, bf16[1,32,2560]{2,1,0:T(8,128)(2,1)}, u32[]{:S(2)}) copy-start(bf16[1,32,2560]{2,1,0:T(8,128)(2,1)} %param.15) | copy-start | bytes 491524
  7.2 98.8 %all-gather.6.cloned.1.call-start = ((), (), s32[]{:S(2)}) async-start(), calls=%async_computation.9 | async-start | bytes 2785280 | tf_op jit(solution)/shard_map/all_gather | solution.py:134
  18.4 142.7 %all-gather.8.cloned.1.call-start = ((), (), s32[]{:S(2)}) async-start(), calls=%async_computation.12 | async-start | bytes 2785280 | tf_op jit(solution)/shard_map/all_gather | solution.py:192
  21.8 12.7 %all-to-all-start.2 = ((bf16[32,4,640]{2,0,1:T(8,128)(2,1)}), bf16[32,4,640]{2,0,1:T(8,128)(2,1)S(1)}, u32[]{:S(2)}, u32[]{:S(2)}) async-start(bf16[32,4,640]{2,0,1:T(8,128)(2,1)} %copy.170), calls=%async_computation.2 | async-start | bytes 327680 | tf_op jit(solution)/shard_map/all_to_all | solution.py:128
  26.6 157.5 %all-gather.10.cloned.1.call-start = ((), (), s32[]{:S(2)}) async-start(), calls=%async_computation.13 | async-start | bytes 2785280 | tf_op jit(solution)/shard_map/all_gather | solution.py:193
  29.9 3.0 copy-start.13
  34.6 9.5 %all-to-all-start = ((bf16[32,4,640]{2,0,1:T(8,128)(2,1)}), bf16[32,4,640]{2,0,1:T(8,128)(2,1)S(1)}, u32[]{:S(2)}, u32[]{:S(2)}) async-start(bf16[32,4,640]{2,0,1:T(8,128)(2,1)} %copy.165), calls=%async_computation | async-start | bytes 327680 | tf_op jit(solution)/shard_map/all_to_all | solution.py:126
  39.4 14.6 %collective-permute-start = (bf16[128,640]{1,0:T(8,128)(2,1)S(1)}, bf16[128,640]{1,0:T(8,128)(2,1)S(1)}, u32[]{:S(2)}, u32[]{:S(2)}) collective-permute-start(bf16[128,640]{1,0:T(8,128)(2,1)S(1)} %bitcast.98), channel_id=1, source_target_pairs={{0,16},{16,32},{32,48},{48,64},{64,80},{80,96},{96,112},{112,128},... | collective-permute-start | bytes 491528 | tf_op jit(solution)/shard_map/ppermute | solution.py:23
  44.1 9.5 %all-to-all-start.3 = ((bf16[32,4,640]{2,0,1:T(8,128)(2,1)}), bf16[32,4,640]{2,0,1:T(8,128)(2,1)S(1)}, u32[]{:S(2)}, u32[]{:S(2)}) async-start(bf16[32,4,640]{2,0,1:T(8,128)(2,1)} %copy.187), calls=%async_computation.3 | async-start | bytes 327680 | tf_op jit(solution)/shard_map/all_to_all | solution.py:129
  48.8 308.2 %reduce-scatter.3.cloned.1.call-start = ((), (), s32[]{:S(2)}) async-start(), calls=%async_computation.10 | async-start | bytes 11141120 | tf_op jit(solution)/shard_map/reduce_scatter | solution.py:161
  49.0 5.4 %collective-permute-start.1 = (bf16[128,640]{1,0:T(8,128)(2,1)S(1)}, bf16[128,640]{1,0:T(8,128)(2,1)}, u32[]{:S(2)}, u32[]{:S(2)}) collective-permute-start(bf16[128,640]{1,0:T(8,128)(2,1)S(1)} %bitcast.100), channel_id=1, source_target_pairs={{0,240},{16,0},{32,16},{48,32},{64,48},{80,64},{96,80},{112,96},{1... | collective-permute-start | bytes 491528 | tf_op jit(solution)/shard_map/ppermute | solution.py:28
  54.1 6.3 %collective-permute-start.2 = (bf16[128,640]{1,0:T(8,128)(2,1)S(1)}, bf16[128,640]{1,0:T(8,128)(2,1)}, u32[]{:S(2)}, u32[]{:S(2)}) collective-permute-start(bf16[128,640]{1,0:T(8,128)(2,1)S(1)} %collective-permute-done), channel_id=1, source_target_pairs={{0,16},{16,32},{32,48},{48,64},{64,80},{80,96},{96,112},{112,128},... | collective-permute-start | bytes 491528 | tf_op jit(solution)/shard_map/ppermute | solution.py:23
  55.5 6.4 %collective-permute-start.3 = (bf16[128,640]{1,0:T(8,128)(2,1)}, bf16[128,640]{1,0:T(8,128)(2,1)S(1)}, u32[]{:S(2)}, u32[]{:S(2)}) collective-permute-start(bf16[128,640]{1,0:T(8,128)(2,1)} %collective-permute-done.1), channel_id=1, source_target_pairs={{0,240},{16,0},{32,16},{48,32},{64,48},{80,64},{96,80},{112,96},{1... | collective-permute-start | bytes 491528 | tf_op jit(solution)/shard_map/ppermute | solution.py:28
  61.5 6.2 %collective-permute-start.4 = (bf16[128,640]{1,0:T(8,128)(2,1)}, bf16[128,640]{1,0:T(8,128)(2,1)S(1)}, u32[]{:S(2)}, u32[]{:S(2)}) collective-permute-start(bf16[128,640]{1,0:T(8,128)(2,1)} %collective-permute-done.2), channel_id=1, source_target_pairs={{0,16},{16,32},{32,48},{48,64},{64,80},{80,96},{96,112},{112,128},... | collective-permute-start | bytes 491528 | tf_op jit(solution)/shard_map/ppermute | solution.py:23
  62.0 5.9 %collective-permute-start.5 = (bf16[128,640]{1,0:T(8,128)(2,1)S(1)}, bf16[128,640]{1,0:T(8,128)(2,1)}, u32[]{:S(2)}, u32[]{:S(2)}) collective-permute-start(bf16[128,640]{1,0:T(8,128)(2,1)S(1)} %collective-permute-done.3), channel_id=1, source_target_pairs={{0,240},{16,0},{32,16},{48,32},{64,48},{80,64},{96,80},{112,96},{1... | collective-permute-start | bytes 491528 | tf_op jit(solution)/shard_map/ppermute | solution.py:28
  67.8 6.1 %collective-permute-start.6 = (bf16[128,640]{1,0:T(8,128)(2,1)S(1)}, bf16[128,640]{1,0:T(8,128)(2,1)}, u32[]{:S(2)}, u32[]{:S(2)}) collective-permute-start(bf16[128,640]{1,0:T(8,128)(2,1)S(1)} %collective-permute-done.4), channel_id=1, source_target_pairs={{0,16},{16,32},{32,48},{48,64},{64,80},{80,96},{96,112},{112,128},... | collective-permute-start | bytes 491528 | tf_op jit(solution)/shard_map/ppermute | solution.py:23
  69.0 7.3 %collective-permute-start.7 = (bf16[128,640]{1,0:T(8,128)(2,1)}, bf16[128,640]{1,0:T(8,128)(2,1)}, u32[]{:S(2)}, u32[]{:S(2)}) collective-permute-start(bf16[128,640]{1,0:T(8,128)(2,1)} %collective-permute-done.5), channel_id=1, source_target_pairs={{0,240},{16,0},{32,16},{48,32},{64,48},{80,64},{96,80},{112,96},{1... | collective-permute-start | bytes 491528 | tf_op jit(solution)/shard_map/ppermute | solution.py:28
  75.0 6.8 %collective-permute-start.8 = (bf16[128,640]{1,0:T(8,128)(2,1)}, bf16[128,640]{1,0:T(8,128)(2,1)S(1)}, u32[]{:S(2)}, u32[]{:S(2)}) collective-permute-start(bf16[128,640]{1,0:T(8,128)(2,1)} %collective-permute-done.6), channel_id=1, source_target_pairs={{0,16},{16,32},{32,48},{48,64},{64,80},{80,96},{96,112},{112,128},... | collective-permute-start | bytes 491528 | tf_op jit(solution)/shard_map/ppermute | solution.py:23
  75.1 34.0 %copy-start.10 = (pred[128,2048]{1,0:T(8,128)(4,1)S(1)}, pred[128,2048]{1,0:T(8,128)(4,1)}, u32[]{:S(2)}) copy-start(pred[128,2048]{1,0:T(8,128)(4,1)} %broadcast_compare_fusion) | copy-start | bytes 786436
  77.4 6.3 %collective-permute-start.9 = (bf16[128,640]{1,0:T(8,128)(2,1)}, bf16[128,640]{1,0:T(8,128)(2,1)}, u32[]{:S(2)}, u32[]{:S(2)}) collective-permute-start(bf16[128,640]{1,0:T(8,128)(2,1)} %collective-permute-done.7), channel_id=1, source_target_pairs={{0,240},{16,0},{32,16},{48,32},{64,48},{80,64},{96,80},{112,96},{1... | collective-permute-start | bytes 491528 | tf_op jit(solution)/shard_map/ppermute | solution.py:28
  81.9 7.0 %collective-permute-start.10 = (bf16[128,640]{1,0:T(8,128)(2,1)S(1)}, bf16[128,640]{1,0:T(8,128)(2,1)}, u32[]{:S(2)}, u32[]{:S(2)}) collective-permute-start(bf16[128,640]{1,0:T(8,128)(2,1)S(1)} %collective-permute-done.8), channel_id=1, source_target_pairs={{0,16},{16,32},{32,48},{48,64},{64,80},{80,96},{96,112},{112,128},... | collective-permute-start | bytes 491528 | tf_op jit(solution)/shard_map/ppermute | solution.py:23
  84.8 7.9 %collective-permute-start.11 = (bf16[128,640]{1,0:T(8,128)(2,1)}, bf16[128,640]{1,0:T(8,128)(2,1)}, u32[]{:S(2)}, u32[]{:S(2)}) collective-permute-start(bf16[128,640]{1,0:T(8,128)(2,1)} %collective-permute-done.9), channel_id=1, source_target_pairs={{0,240},{16,0},{32,16},{48,32},{64,48},{80,64},{96,80},{112,96},{1... | collective-permute-start | bytes 491528 | tf_op jit(solution)/shard_map/ppermute | solution.py:28
  90.0 7.0 %collective-permute-start.12 = (bf16[128,640]{1,0:T(8,128)(2,1)}, bf16[128,640]{1,0:T(8,128)(2,1)S(1)}, u32[]{:S(2)}, u32[]{:S(2)}) collective-permute-start(bf16[128,640]{1,0:T(8,128)(2,1)} %collective-permute-done.10), channel_id=1, source_target_pairs={{0,16},{16,32},{32,48},{48,64},{64,80},{80,96},{96,112},{112,128},... | collective-permute-start | bytes 491528 | tf_op jit(solution)/shard_map/ppermute | solution.py:23
  93.8 8.0 %collective-permute-start.13 = (bf16[128,640]{1,0:T(8,128)(2,1)}, bf16[128,640]{1,0:T(8,128)(2,1)}, u32[]{:S(2)}, u32[]{:S(2)}) collective-permute-start(bf16[128,640]{1,0:T(8,128)(2,1)} %collective-permute-done.11), channel_id=1, source_target_pairs={{0,240},{16,0},{32,16},{48,32},{64,48},{80,64},{96,80},{112,96},{1... | collective-permute-start | bytes 491528 | tf_op jit(solution)/shard_map/ppermute | solution.py:28
  97.2 6.1 %collective-permute-start.14 = (bf16[128,640]{1,0:T(8,128)(2,1)S(1)}, bf16[128,640]{1,0:T(8,128)(2,1)}, u32[]{:S(2)}, u32[]{:S(2)}) collective-permute-start(bf16[128,640]{1,0:T(8,128)(2,1)S(1)} %collective-permute-done.12), channel_id=1, source_target_pairs={{0,16},{16,32},{32,48},{48,64},{64,80},{80,96},{96,112},{112,128},... | collective-permute-start | bytes 491528 | tf_op jit(solution)/shard_map/ppermute | solution.py:23
  103.3 5.7 %copy-start.16 = (f32[5]{0:T(128)S(1)}, f32[5]{0:T(128)}, u32[]{:S(2)}) copy-start(f32[5]{0:T(128)} %get-tuple-element.83) | copy-start | bytes 64
  103.3 5.7 %copy-start.17 = (f32[5]{0:T(128)S(1)}, f32[5]{0:T(128)}, u32[]{:S(2)}) copy-start(f32[5]{0:T(128)} %get-tuple-element.84) | copy-start | bytes 64
  104.5 1.5 copy-start.7
  109.0 4.5 %copy-start.3 = (bf16[2048,640]{0,1:T(8,128)(2,1)}, bf16[2048,640]{0,1:T(8,128)(2,1)S(1)}, u32[]{:S(2)}) copy-start(bf16[2048,640]{0,1:T(8,128)(2,1)S(1)} %copy.167) | copy-start | bytes 7864324
  113.6 3.9 %copy-start.4 = (f32[5,128,2048]{2,1,0:T(8,128)}, f32[5,128,2048]{2,1,0:T(8,128)S(1)}, u32[]{:S(2)}) copy-start(f32[5,128,2048]{2,1,0:T(8,128)S(1)} %select_add_fusion) | copy-start | bytes 15728644
  125.4 6.1 %copy-start.8 = (bf16[2048,640]{0,1:T(8,128)(2,1)S(1)}, bf16[2048,640]{0,1:T(8,128)(2,1)}, u32[]{:S(2)}) copy-start(bf16[2048,640]{0,1:T(8,128)(2,1)} %copy-done.7) | copy-start | bytes 7864324
  131.4 3.8 copy-start.5
  131.4 3.8 copy-start.6
  157.2 1.0 copy-start.9
  157.2 2.3 copy-start.14
  157.2 207.7 %reduce-scatter.5.cloned.1.call-start = ((), (), s32[]{:S(2)}) async-start(), calls=%async_computation.11 | async-start | bytes 11141120 | tf_op jit(solution)/shard_map/reduce_scatter | solution.py:223
  184.1 6.3 %slice-start = ((s8[10485760]{0:T(1024)(128)(4,1)}), s8[4194304]{0:T(1024)(128)(4,1)S(1)}, s32[]{:S(2)}) async-start(s8[10485760]{0:T(1024)(128)(4,1)} %bitcast.88), calls=%async_computation.14 | async-start | bytes 8388608
  184.1 7.6 %slice-start.1 = ((s8[10485760]{0:T(1024)(128)(4,1)}), s8[4194304]{0:T(1024)(128)(4,1)S(1)}, s32[]{:S(2)}) async-start(s8[10485760]{0:T(1024)(128)(4,1)} %bitcast.88), calls=%async_computation.15 | async-start | bytes 8388608
  184.1 8.3 %slice-start.2 = ((s8[10485760]{0:T(1024)(128)(4,1)}), s8[2097152]{0:T(1024)(128)(4,1)S(1)}, s32[]{:S(2)}) async-start(s8[10485760]{0:T(1024)(128)(4,1)} %bitcast.88), calls=%async_computation.16 | async-start | bytes 4194304
  194.2 3.9 %copy-start.2 = (bf16[5,256,2048]{2,1,0:T(8,128)(2,1)}, bf16[5,256,2048]{2,1,0:T(8,128)(2,1)S(1)}, u32[]{:S(2)}) copy-start(bf16[5,256,2048]{2,1,0:T(8,128)(2,1)S(1)} %multiply_convert_fusion) | copy-start | bytes 15728644
  218.2 160.3 %copy-start.1 = (s32[1,4096]{1,0:T(1,128)S(1)}, s32[1,4096]{1,0:T(1,128)}, u32[]{:S(2)}) copy-start(s32[1,4096]{1,0:T(1,128)} %param.23) | copy-start | bytes 49156
  222.8 136.1 %all-to-all-start.4 = ((bf16[4,32,640]{2,1,0:T(8,128)(2,1)}), bf16[4,32,640]{2,1,0:T(8,128)(2,1)S(1)}, u32[]{:S(2)}, u32[]{:S(2)}) async-start(bf16[4,32,640]{2,1,0:T(8,128)(2,1)} %convert_element_type.95), calls=%async_computation.4 | async-start | bytes 327680 | tf_op jit(solution)/shard_map/all_to_all | solution.py:176
  358.9 9.4 %all-to-all-start.5 = ((bf16[4,32,640]{2,1,0:T(8,128)(2,1)}), bf16[4,32,640]{2,1,0:T(8,128)(2,1)S(1)}, u32[]{:S(2)}, u32[]{:S(2)}) async-start(bf16[4,32,640]{2,1,0:T(8,128)(2,1)} %bitcast.23), calls=%async_computation.6 | async-start | bytes 327680 | tf_op jit(solution)/shard_map/all_to_all | solution.py:183
  368.3 9.5 %all-to-all-start.6 = ((bf16[4,32,640]{2,1,0:T(8,128)(2,1)}), bf16[4,32,640]{2,1,0:T(8,128)(2,1)S(1)}, u32[]{:S(2)}, u32[]{:S(2)}) async-start(bf16[4,32,640]{2,1,0:T(8,128)(2,1)} %bitcast.25), calls=%async_computation.7 | async-start | bytes 327680 | tf_op jit(solution)/shard_map/all_to_all | solution.py:186
Sparse Core Ops, SparseCore 0:
  18.5 42.1 all-gather.5
  63.1 44.1 all-gather.7
  109.7 42.4 all-gather.9
  157.4 79.9 reduce-scatter.2
  239.7 74.3 reduce-scatter.4
